TPU v7x, 32 devices: a whole 2x2x4 slice. The times are simulated.
32 devices in a mesh: ctx: 4 (over y, x), fsdp: 8 (over z, core).
Axes of the slice: x: 2, y: 2, z: 4, core: 2. Of those that a mesh axis runs over, the one named last changes fastest.
Arguments:
- tokens: bfloat16 [8, 4, 2, 256, 1024], P('fsdp', 'ctx'), may hold values from -6 to 6
- cotangent: bfloat16 [8, 4, 2, 256, 1024], P('fsdp', 'ctx'), may hold values from -6 to 6
- block_pair: int32 [4], replicated, may hold values from 0 to 3, each once
- segment_ids: int32 [8, 2048], P('fsdp'), may hold values from 0 to 2, as said below
- attn_gain: float32 [1024], replicated, may hold values from 0.5 to 1.5
- query_gain: float32 [64], replicated, may hold values from 0.5 to 1.5
- key_gain: float32 [64], replicated, may hold values from 0.5 to 1.5
- ffn_gain: float32 [1024], replicated, may hold values from 0.5 to 1.5
- w_query: bfloat16 [1024, 1024], P('fsdp'), may hold values from -0.1875 to 0.1875
- w_key: bfloat16 [1024, 512], P('fsdp'), may hold values from -0.1875 to 0.1875
- w_value: bfloat16 [1024, 512], P('fsdp'), may hold values from -0.1875 to 0.1875
- w_output: bfloat16 [1024, 1024], P('fsdp'), may hold values from -4 to 4
- w_gate: bfloat16 [1024, 4608], P('fsdp'), may hold values from -0.1875 to 0.1875
- w_up: bfloat16 [1024, 4608], P('fsdp'), may hold values from -0.1875 to 0.1875
- w_down: bfloat16 [4608, 1024], P('fsdp'), may hold values from -0.09375 to 0.09375
Outputs:
- output: bfloat16 [8, 4, 2, 256, 1024], P('fsdp', 'ctx')
- input_grad: float32 [8, 4, 2, 256, 1024], P('fsdp', 'ctx')
- attn_gain_grad: float32 [1024], P(('ctx', 'fsdp'))
- query_gain_grad: float32 [64], replicated
- key_gain_grad: float32 [64], replicated
- ffn_gain_grad: float32 [1024], P(('ctx', 'fsdp'))
- w_query_grad: float32 [1024, 1024], P(('ctx', 'fsdp'))
- w_key_grad: float32 [1024, 512], P(('ctx', 'fsdp'))
- w_value_grad: float32 [1024, 512], P(('ctx', 'fsdp'))
- w_output_grad: float32 [1024, 1024], P(('ctx', 'fsdp'))
- w_gate_grad: float32 [1024, 4608], P(('ctx', 'fsdp'))
- w_up_grad: float32 [1024, 4608], P(('ctx', 'fsdp'))
- w_down_grad: float32 [4608, 1024], P(('ctx', 'fsdp'))
Inputs may be any that keep to these rules, and one draw needn't show every extreme that they name: `block_pair`: each ctx index holds a different pair of blocks. `segment_ids`: never falling along a sequence; document 0 starts each sequence and covers at least its first 1024 positions.
All inputs are finite; a program needn't handle non-finite values.
Results may differ from a plain program's by a relative error of at most 0.023.
Values may be sent and summed in bfloat16 or wider, within the bound.
A program may use at most 192 MiB of HBM per device.

v0:
```python
import math

import jax
import jax.numpy as jnp
from jax import lax
from jax.sharding import PartitionSpec as P

Q_HEADS = 16
KV_HEADS = 8
HEAD_DIM = 64


EPSILON = 1e-05
ROPE_THETA = 1000000.0
MASKED_SCORE = -1e30


def norm_parts(value, gain):
    factor = lax.rsqrt(jnp.mean(value * value, axis=-1, keepdims=True) + EPSILON)
    normal = value * factor
    return (normal * gain, normal, factor)


def norm_back(grad_in, normal, factor, gain):
    inner = grad_in * gain
    back = factor * (inner - normal * jnp.mean(inner * normal, axis=-1, keepdims=True))
    return (back, grad_in * normal)


def turn_half(value):
    middle = value.shape[-1] // 2
    return jnp.concatenate([-value[..., middle:], value[..., :middle]], axis=-1)


def turn_back(value):
    middle = value.shape[-1] // 2
    return jnp.concatenate([value[..., middle:], -value[..., :middle]], axis=-1)


def angles(positions, head_size):
    middle = head_size // 2
    freqs = ROPE_THETA ** (-jnp.arange(middle, dtype=jnp.float32) * 2.0 / head_size)
    phase = positions.astype(jnp.float32)[:, None] * freqs[None, :]
    phase = jnp.concatenate([phase, phase], axis=-1)
    return (jnp.cos(phase)[:, None, :], jnp.sin(phase)[:, None, :])


def contract_rows(left, right):
    return lax.dot_general(
        left, right, (((0,), (0,)), ((), ())), preferred_element_type=jnp.float32
    )


def times_transposed(left, right):
    return lax.dot_general(
        left, right, (((1,), (1,)), ((), ())), preferred_element_type=jnp.float32
    )


def shards(
    tokens,
    cotangent,
    block_pair,
    segment_ids,
    attn_gain,
    query_gain,
    key_gain,
    ffn_gain,
    w_query,
    w_key,
    w_value,
    w_output,
    w_gate,
    w_up,
    w_down,
):
    ctx_count = lax.axis_size("ctx")
    ctx_rank = lax.axis_index("ctx")
    block_len = tokens.shape[3]
    model_width = tokens.shape[4]
    local_rows = 2 * block_len
    seq_rows = 2 * ctx_count * block_len
    group_size = Q_HEADS // KV_HEADS
    score_scale = HEAD_DIM ** (-0.5)
    blocks = jnp.stack([block_pair, 2 * ctx_count - 1 - block_pair], axis=1).reshape(-1)
    key_pos = (
        blocks[:, None] * block_len + jnp.arange(block_len, dtype=jnp.int32)[None, :]
    ).reshape(-1)
    key_seg = jnp.take(segment_ids.reshape(2 * ctx_count, block_len), blocks, axis=0).reshape(-1)
    own_pos = lax.dynamic_slice_in_dim(key_pos, ctx_rank * local_rows, local_rows)
    own_seg = lax.dynamic_slice_in_dim(key_seg, ctx_rank * local_rows, local_rows)
    cosine, sine_part = angles(own_pos, HEAD_DIM)
    inputs_now = tokens.reshape(local_rows, model_width).astype(jnp.float32)
    full_query, full_key, full_value, full_output, full_gate, full_up, full_down = (
        lax.all_gather(w_query, "fsdp", axis=0, tiled=True),
        lax.all_gather(w_key, "fsdp", axis=0, tiled=True),
        lax.all_gather(w_value, "fsdp", axis=0, tiled=True),
        lax.all_gather(w_output, "fsdp", axis=0, tiled=True),
        lax.all_gather(w_gate, "fsdp", axis=0, tiled=True),
        lax.all_gather(w_up, "fsdp", axis=0, tiled=True),
        lax.all_gather(w_down, "fsdp", axis=0, tiled=True),
    )
    attn_out, attn_normal, attn_factor = norm_parts(inputs_now, attn_gain)
    attn_in = attn_out.astype(jnp.bfloat16)
    query_raw = jnp.dot(attn_in, full_query, preferred_element_type=jnp.float32).reshape(
        local_rows, Q_HEADS, HEAD_DIM
    )
    key_raw = jnp.dot(attn_in, full_key, preferred_element_type=jnp.float32).reshape(
        local_rows, KV_HEADS, HEAD_DIM
    )
    value_low = jnp.dot(attn_in, full_value, preferred_element_type=jnp.float32).astype(
        jnp.bfloat16
    )
    query_gained, query_normal, query_factor = norm_parts(query_raw, query_gain)
    key_gained, key_normal, key_factor = norm_parts(key_raw, key_gain)
    query_low = (query_gained * cosine + turn_half(query_gained) * sine_part).astype(jnp.bfloat16)
    query_low = query_low.reshape(local_rows, KV_HEADS, group_size, HEAD_DIM)
    key_low = (key_gained * cosine + turn_half(key_gained) * sine_part).astype(jnp.bfloat16)
    key_low = key_low.reshape(local_rows, KV_HEADS * HEAD_DIM)

    def scores_for(key_block, first_key, block_size):
        block_pos = lax.dynamic_slice_in_dim(key_pos, first_key, block_size)
        block_seg = lax.dynamic_slice_in_dim(key_seg, first_key, block_size)
        allowed = (block_pos[None, :] <= own_pos[:, None]) & (
            block_seg[None, :] == own_seg[:, None]
        )
        raw_scores = (
            jnp.einsum(
                "qhgd,khd->qhgk",
                query_low,
                key_block.reshape(block_size, KV_HEADS, HEAD_DIM),
                preferred_element_type=jnp.float32,
            )
            * score_scale
        )
        allowed = allowed[:, None, None, :]
        return (jnp.where(allowed, raw_scores, MASKED_SCORE), allowed)

    start_state = (
        jnp.full((local_rows, KV_HEADS, group_size), MASKED_SCORE, jnp.float32),
        jnp.zeros((local_rows, KV_HEADS, group_size), jnp.float32),
        jnp.zeros((local_rows, KV_HEADS, group_size, HEAD_DIM), jnp.float32),
    )
    key_rows = lax.all_gather(key_low, "ctx", axis=0, tiled=True)
    value_rows = lax.all_gather(value_low, "ctx", axis=0, tiled=True)
    block_size = math.gcd(key_rows.shape[0], 256)

    def forward_advance(block_index, running_now):
        peak, denom_sum, weighted = running_now
        offset = block_index * block_size
        key_block = lax.dynamic_slice_in_dim(key_rows, offset, block_size)
        value_block = lax.dynamic_slice_in_dim(value_rows, offset, block_size).reshape(
            block_size, KV_HEADS, HEAD_DIM
        )
        masked, allowed = scores_for(key_block, offset, block_size)
        new_peak = jnp.maximum(peak, jnp.max(masked, axis=-1))
        attn_probs = jnp.where(allowed, jnp.exp(masked - new_peak[..., None]), 0.0)
        shrink = jnp.exp(peak - new_peak)
        denom_sum = denom_sum * shrink + jnp.sum(attn_probs, axis=-1)
        weighted = weighted * shrink[..., None] + jnp.einsum(
            "qhgk,khd->qhgd",
            attn_probs.astype(jnp.bfloat16),
            value_block,
            preferred_element_type=jnp.float32,
        )
        return (new_peak, denom_sum, weighted)

    peak, denom_sum, weighted = lax.fori_loop(
        0, key_rows.shape[0] // block_size, forward_advance, start_state
    )
    log_total = peak + jnp.log(denom_sum)
    attn_mix = weighted / denom_sum[..., None]
    mixed_low = attn_mix.reshape(local_rows, Q_HEADS * HEAD_DIM).astype(jnp.bfloat16)
    residual = inputs_now + jnp.dot(mixed_low, full_output, preferred_element_type=jnp.float32)
    ffn_out, ffn_normal, ffn_factor = norm_parts(residual, ffn_gain)
    ffn_in = ffn_out.astype(jnp.bfloat16)
    gate_value = jnp.dot(ffn_in, full_gate, preferred_element_type=jnp.float32)
    up_value = jnp.dot(ffn_in, full_up, preferred_element_type=jnp.float32)
    gate_sigmoid = jax.nn.sigmoid(gate_value)
    gate_silu = gate_value * gate_sigmoid
    activation = (gate_silu * up_value).astype(jnp.bfloat16)
    result = residual + jnp.dot(activation, full_down, preferred_element_type=jnp.float32)
    output = result.astype(jnp.bfloat16).reshape(tokens.shape)
    grad_low = cotangent.reshape(local_rows, model_width)
    down_wgrad = contract_rows(activation, grad_low)
    act_grad = times_transposed(grad_low, full_down)
    gate_grad = (
        act_grad * up_value * gate_sigmoid * (1.0 + gate_value * (1.0 - gate_sigmoid))
    ).astype(jnp.bfloat16)
    up_grad = (act_grad * gate_silu).astype(jnp.bfloat16)
    gate_wgrad = contract_rows(ffn_in, gate_grad)
    up_wgrad = contract_rows(ffn_in, up_grad)
    ffn_in_grad = times_transposed(gate_grad, full_gate) + times_transposed(up_grad, full_up)
    ffn_back, ffn_gain_part = norm_back(ffn_in_grad, ffn_normal, ffn_factor, ffn_gain)
    ffn_gain_wgrad = jnp.sum(ffn_gain_part, axis=0)
    residual_grad = grad_low.astype(jnp.float32) + ffn_back
    gate_sum, up_sum, down_sum, ffn_gain_sum = (
        lax.psum_scatter(gate_wgrad, ("ctx", "fsdp"), scatter_dimension=0, tiled=True),
        lax.psum_scatter(up_wgrad, ("ctx", "fsdp"), scatter_dimension=0, tiled=True),
        lax.psum_scatter(down_wgrad, ("ctx", "fsdp"), scatter_dimension=0, tiled=True),
        lax.psum_scatter(ffn_gain_wgrad, ("ctx", "fsdp"), scatter_dimension=0, tiled=True),
    )
    residual_low = residual_grad.astype(jnp.bfloat16)
    output_wgrad = contract_rows(mixed_low, residual_low)
    mixed_grad = times_transposed(residual_low, full_output).astype(jnp.bfloat16)
    mixed_grad = mixed_grad.reshape(local_rows, KV_HEADS, group_size, HEAD_DIM)
    row_delta = jnp.sum(mixed_grad.astype(jnp.float32) * attn_mix, axis=-1)
    back_state = (
        jnp.zeros((local_rows, KV_HEADS, group_size, HEAD_DIM), jnp.float32),
        jnp.zeros((seq_rows, KV_HEADS * HEAD_DIM), jnp.float32),
        jnp.zeros((seq_rows, KV_HEADS * HEAD_DIM), jnp.float32),
    )
    backward_key_rows = lax.all_gather(key_low, "ctx", axis=0, tiled=True)
    backward_value_rows = lax.all_gather(value_low, "ctx", axis=0, tiled=True)
    backward_block_size = math.gcd(backward_key_rows.shape[0], 256)

    def backward_advance(block_index, running_now):
        query_grad, key_grad_all, value_grad_all = running_now
        offset = block_index * backward_block_size
        key_block = lax.dynamic_slice_in_dim(backward_key_rows, offset, backward_block_size)
        value_block = lax.dynamic_slice_in_dim(
            backward_value_rows, offset, backward_block_size
        ).reshape(backward_block_size, KV_HEADS, HEAD_DIM)
        masked, allowed = scores_for(key_block, offset, backward_block_size)
        attn_probs = jnp.where(allowed, jnp.exp(masked - log_total[..., None]), 0.0)
        value_part = jnp.einsum(
            "qhgk,qhgd->khd",
            attn_probs.astype(jnp.bfloat16),
            mixed_grad,
            preferred_element_type=jnp.float32,
        )
        prob_grad = jnp.einsum(
            "qhgd,khd->qhgk", mixed_grad, value_block, preferred_element_type=jnp.float32
        )
        score_grad = (attn_probs * (prob_grad - row_delta[..., None])).astype(jnp.bfloat16)
        query_grad = (
            query_grad
            + jnp.einsum(
                "qhgk,khd->qhgd",
                score_grad,
                key_block.reshape(backward_block_size, KV_HEADS, HEAD_DIM),
                preferred_element_type=jnp.float32,
            )
            * score_scale
        )
        key_part = (
            jnp.einsum("qhgk,qhgd->khd", score_grad, query_low, preferred_element_type=jnp.float32)
            * score_scale
        )
        key_grad_all = lax.dynamic_update_slice_in_dim(
            key_grad_all,
            lax.dynamic_slice_in_dim(key_grad_all, offset, backward_block_size)
            + key_part.reshape(backward_block_size, KV_HEADS * HEAD_DIM),
            offset,
            0,
        )
        value_grad_all = lax.dynamic_update_slice_in_dim(
            value_grad_all,
            lax.dynamic_slice_in_dim(value_grad_all, offset, backward_block_size)
            + value_part.reshape(backward_block_size, KV_HEADS * HEAD_DIM),
            offset,
            0,
        )
        return (query_grad, key_grad_all, value_grad_all)

    query_grad, key_grad_all, value_grad_all = lax.fori_loop(
        0, backward_key_rows.shape[0] // backward_block_size, backward_advance, back_state
    )
    key_grad, value_grad = (
        lax.psum_scatter(
            key_grad_all.astype(jnp.bfloat16), "ctx", scatter_dimension=0, tiled=True
        ).astype(jnp.float32),
        lax.psum_scatter(
            value_grad_all.astype(jnp.bfloat16), "ctx", scatter_dimension=0, tiled=True
        ).astype(jnp.float32),
    )
    key_grad = key_grad.reshape(local_rows, KV_HEADS, HEAD_DIM)
    key_turned = key_grad * cosine + turn_back(key_grad * sine_part)
    key_back, key_gain_part = norm_back(key_turned, key_normal, key_factor, key_gain)
    key_gain_local = jnp.sum(key_gain_part, axis=(0, 1))
    key_raw_grad = key_back.reshape(local_rows, KV_HEADS * HEAD_DIM).astype(jnp.bfloat16)
    query_grad = query_grad.reshape(local_rows, Q_HEADS, HEAD_DIM)
    query_turned = query_grad * cosine + turn_back(query_grad * sine_part)
    query_back, query_gain_part = norm_back(query_turned, query_normal, query_factor, query_gain)
    query_gain_local = jnp.sum(query_gain_part, axis=(0, 1))
    query_raw_grad = query_back.reshape(local_rows, Q_HEADS * HEAD_DIM).astype(jnp.bfloat16)
    value_raw_grad = value_grad.astype(jnp.bfloat16)
    query_wgrad = contract_rows(attn_in, query_raw_grad)
    key_wgrad = contract_rows(attn_in, key_raw_grad)
    value_wgrad = contract_rows(attn_in, value_raw_grad)
    attn_in_grad = (
        times_transposed(query_raw_grad, full_query)
        + times_transposed(key_raw_grad, full_key)
        + times_transposed(value_raw_grad, full_value)
    )
    attn_back, attn_gain_part = norm_back(attn_in_grad, attn_normal, attn_factor, attn_gain)
    attn_gain_wgrad = jnp.sum(attn_gain_part, axis=0)
    input_grad = (residual_grad + attn_back).reshape(tokens.shape)
    query_sum, key_sum, value_sum, output_sum, attn_gain_sum = (
        lax.psum_scatter(query_wgrad, ("ctx", "fsdp"), scatter_dimension=0, tiled=True),
        lax.psum_scatter(key_wgrad, ("ctx", "fsdp"), scatter_dimension=0, tiled=True),
        lax.psum_scatter(value_wgrad, ("ctx", "fsdp"), scatter_dimension=0, tiled=True),
        lax.psum_scatter(output_wgrad, ("ctx", "fsdp"), scatter_dimension=0, tiled=True),
        lax.psum_scatter(attn_gain_wgrad, ("ctx", "fsdp"), scatter_dimension=0, tiled=True),
    )
    query_gain_sum, key_gain_sum = lax.psum((query_gain_local, key_gain_local), ("ctx", "fsdp"))
    return (
        output,
        input_grad,
        attn_gain_sum,
        query_gain_sum,
        key_gain_sum,
        ffn_gain_sum,
        query_sum,
        key_sum,
        value_sum,
        output_sum,
        gate_sum,
        up_sum,
        down_sum,
    )


def solution(mesh):
    placed = (
        P("fsdp", "ctx", None, None, None),
        P("fsdp", "ctx", None, None, None),
        P(),
        P("fsdp", None),
        P(),
        P(),
        P(),
        P(),
        P("fsdp", None),
        P("fsdp", None),
        P("fsdp", None),
        P("fsdp", None),
        P("fsdp", None),
        P("fsdp", None),
        P("fsdp", None),
    )
    return jax.shard_map(
        shards,
        mesh=mesh,
        in_specs=placed,
        out_specs=(
            P("fsdp", "ctx", None, None, None),
            P("fsdp", "ctx", None, None, None),
            P(("ctx", "fsdp")),
            P(),
            P(),
            P(("ctx", "fsdp")),
            P(("ctx", "fsdp"), None),
            P(("ctx", "fsdp"), None),
            P(("ctx", "fsdp"), None),
            P(("ctx", "fsdp"), None),
            P(("ctx", "fsdp"), None),
            P(("ctx", "fsdp"), None),
            P(("ctx", "fsdp"), None),
        ),
        check_vma=False,
    )
```

profile of v0, /device:TPU:0, one launch (start us, length us, event | category | flops | bytes accessed | tf_op | source)
XLA Modules:
  0.0 1942.3 jit_solution(7755589778545727779)
XLA Ops:
  12.6 21.9 %all-gather.16.cloned.1.call-done = bf16[1024,512]{1,0:T(8,128)(2,1)} async-done(((bf16[128,512]{1,0:T(8,128)(2,1)}), bf16[1024,512]{1,0:T(8,128)(2,1)}) %all-gather.16.cloned.1.call-update) | async-done | bytes 1048592 | tf_op jit(solution)/shard_map/all_gather | solution.py:97
  38.4 19.5 %all-gather.10.cloned.1.call-done = bf16[1024,512]{1,0:T(8,128)(2,1)} async-done(((bf16[128,512]{1,0:T(8,128)(2,1)}), bf16[1024,512]{1,0:T(8,128)(2,1)}) %all-gather.10.cloned.1.call-update) | async-done | bytes 1048592 | tf_op jit(solution)/shard_map/all_gather | solution.py:96
  69.0 19.2 all-gather.14.cloned.1.call-done
  97.2 28.2 %all-gather.18.cloned.1.call-done = bf16[2048,512]{1,0:T(8,128)(2,1)} async-done(((bf16[512,512]{1,0:T(8,128)(2,1)}), bf16[2048,512]{1,0:T(8,128)(2,1)}) %all-gather.18.cloned.1.call-update) | async-done | bytes 2097168 | tf_op jit(solution)/shard_map/all_gather | solution.py:145
  129.3 33.5 %all-gather.12.cloned.1.call-done = bf16[2048,512]{0,1:T(8,128)(2,1)} async-done(((bf16[512,512]{0,1:T(8,128)(2,1)}), bf16[2048,512]{0,1:T(8,128)(2,1)}) %all-gather.12.cloned.1.call-update) | async-done | bytes 2097168 | tf_op jit(solution)/shard_map/all_gather | solution.py:144
  162.8 155.3 %while.36 = (s32[]{:T(128)}, f32[512,8,2]{0,2,1:T(2,128)}, f32[512,8,2]{0,2,1:T(2,128)}, f32[512,8,2,64]{0,3,2,1:T(8,128)}, s32[2048]{0:T(1024)S(1)}, /*index=5*...) while((s32[]{:T(128)}, f32[512,8,2]{0,2,1:T(2,128)}, ...), condition=%wide.region_6.7_spmd.clone, body=%wide.region_3.0_spmd.clone.sunk | while | flops 566140928 | bytes 66988352 | solution.py:168
  164.9 5.5 fusion.146
  171.1 4.8 fusion.148
  183.2 5.4 fusion.146
  189.5 4.7 fusion.148
  202.7 5.4 fusion.146
  209.0 4.7 fusion.148
  215.0 4.5 bitcast_add_fusion.7
  222.2 5.5 fusion.146
  228.5 4.7 fusion.148
  234.5 4.5 bitcast_add_fusion.7
  241.7 5.4 fusion.146
  248.0 4.7 fusion.148
  254.0 4.6 bitcast_add_fusion.7
  261.3 5.4 fusion.146
  267.6 4.6 fusion.148
  280.7 5.4 fusion.146
  287.0 4.6 fusion.148
  293.2 4.6 bitcast_add_fusion.7
  300.6 5.5 fusion.146
  306.9 4.7 fusion.148
  327.1 10.1 fusion.57
  337.2 39.0 %all-gather.24.cloned.1.call-done = bf16[1024,4608]{1,0:T(8,128)(2,1)} async-done(((bf16[128,4608]{1,0:T(8,128)(2,1)}), bf16[1024,4608]{1,0:T(8,128)(2,1)}) %all-gather.24.cloned.1.call-update) | async-done | bytes 9437200 | tf_op jit(solution)/shard_map/all_gather | solution.py:100
  376.1 10.5 fusion.58
  386.6 80.4 %all-gather.26.cloned.1.call-done = bf16[4608,1024]{1,0:T(8,128)(2,1)} async-done(((bf16[576,1024]{1,0:T(8,128)(2,1)}), bf16[4608,1024]{1,0:T(8,128)(2,1)}) %all-gather.26.cloned.1.call-update) | async-done | bytes 9437200 | tf_op jit(solution)/shard_map/all_gather | solution.py:101
  467.0 18.0 multiply_convert_fusion
  485.0 9.2 fusion.59
  494.2 8.7 multiply_reduce_fusion
  516.6 146.3 %while.37 = (s32[]{:T(128)}, f32[512,8,2,64]{0,3,2,1:T(8,128)S(1)}, f32[2048,512]{0,1:T(8,128)}, f32[2048,512]{0,1:T(8,128)}, bf16[2048,512]{0,1:T(8,128)(2,1)},...) while((s32[]{:T(128)}, f32[512,8,2,64]{0,3,2,1:T(8,128)S(1)}, ...), condition=%wide.region_11.12_spmd.clone, body=%wide.region_10.11_spmd.clone.sunk | while | flops 1369702400 | bytes 73640232 | solution.py:266
  685.1 15.4 reduce-scatter.10.cloned.1.call-done
  706.0 33.6 %reduce-scatter.12.cloned.1.call-done = bf16[512,512]{0,1:T(8,128)(2,1)} async-done(((bf16[2048,512]{0,1:T(8,128)(2,1)}), bf16[512,512]{0,1:T(8,128)(2,1)}) %reduce-scatter.12.cloned.1.call-update) | async-done | bytes 524304 | tf_op jit(solution)/shard_map/reduce_scatter | solution.py:273
  743.1 11.5 fusion.65
  754.7 11.6 fusion.66
  767.5 11.4 fusion.67
  783.3 9.9 add_convert_fusion
  797.6 40.1 %all-reduce.2 = (f32[1024]{0:T(1024)S(1)}, f32[64]{0:T(128)}, f32[64]{0:T(128)}, f32[1024]{0:T(1024)S(1)}) all-reduce(f32[1024]{0:T(1024)S(1)} %get-tuple-element.596, f32[64]{0:T(128)S(1)} %get-tuple-element.592, f32[64]{0:T(128)S(1)} %get-tuple-element.598, ...), channel_id=4, replica_groups=mesh['ctx'=4,'fsdp'=8] {'ctx','fsdp'}, use_global_device_ids=true, to_apply=%region_18.19.clone | all-reduce | flops 2176 | bytes 17408
  842.2 42.8 %reduce-scatter.14.cloned.1.call-done = f32[32,1024]{1,0:T(8,128)} async-done(((f32[1024,1024]{1,0:T(8,128)}), f32[32,1024]{1,0:T(8,128)}) %reduce-scatter.14.cloned.1.call-update) | async-done | bytes 131088 | tf_op jit(solution)/shard_map/reduce_scatter | solution.py:300
  885.1 142.4 %reduce-scatter.20.cloned.1.call-done = f32[32,1024]{1,0:T(8,128)} async-done(((f32[1024,1024]{1,0:T(8,128)}), f32[32,1024]{1,0:T(8,128)}) %reduce-scatter.20.cloned.1.call-update) | async-done | bytes 131088 | tf_op jit(solution)/shard_map/reduce_scatter | solution.py:303
  1027.5 136.7 %reduce-scatter.16.cloned.1.call-done = f32[32,512]{1,0:T(8,128)} async-done(((f32[1024,512]{1,0:T(8,128)}), f32[32,512]{1,0:T(8,128)}) %reduce-scatter.16.cloned.1.call-update) | async-done | bytes 65552 | tf_op jit(solution)/shard_map/reduce_scatter | solution.py:301
  1164.1 135.8 %reduce-scatter.18.cloned.1.call-done = f32[32,512]{1,0:T(8,128)} async-done(((f32[1024,512]{1,0:T(8,128)}), f32[32,512]{1,0:T(8,128)}) %reduce-scatter.18.cloned.1.call-update) | async-done | bytes 65552 | tf_op jit(solution)/shard_map/reduce_scatter | solution.py:302
  1299.9 210.4 %reduce-scatter.22.cloned.1.call-done = f32[32,4608]{1,0:T(8,128)} async-done(((f32[1024,4608]{1,0:T(8,128)}), f32[32,4608]{1,0:T(8,128)}) %reduce-scatter.22.cloned.1.call-update) | async-done | bytes 589840 | tf_op jit(solution)/shard_map/reduce_scatter | solution.py:198
  1510.2 212.5 %reduce-scatter.24.cloned.1.call-done = f32[32,4608]{1,0:T(8,128)} async-done(((f32[1024,4608]{1,0:T(8,128)}), f32[32,4608]{1,0:T(8,128)}) %reduce-scatter.24.cloned.1.call-update) | async-done | bytes 589840 | tf_op jit(solution)/shard_map/reduce_scatter | solution.py:199
  1722.7 212.5 %reduce-scatter.26.cloned.1.call-done = f32[144,1024]{1,0:T(8,128)} async-done(((f32[4608,1024]{1,0:T(8,128)}), f32[144,1024]{1,0:T(8,128)}) %reduce-scatter.26.cloned.1.call-update) | async-done | bytes 589840 | tf_op jit(solution)/shard_map/reduce_scatter | solution.py:200
  (464 shorter events, 301.6 us)
Async XLA Ops:
  7.2 27.3 %all-gather.16.cloned.1.call-start = ((), (), s32[]{:S(2)}) async-start(), calls=%async_computation.12 | async-start | bytes 1179648 | tf_op jit(solution)/shard_map/all_gather | solution.py:97
  7.9 49.9 %all-gather.10.cloned.1.call-start = ((), (), s32[]{:S(2)}) async-start(), calls=%async_computation.9 | async-start | bytes 1179648 | tf_op jit(solution)/shard_map/all_gather | solution.py:96
  8.7 79.5 %all-gather.14.cloned.1.call-start = ((), (), s32[]{:S(2)}) async-start(), calls=%async_computation.11 | async-start | bytes 2359296 | tf_op jit(solution)/shard_map/all_gather | solution.py:95
  9.4 115.9 %all-gather.18.cloned.1.call-start = ((), (), s32[]{:S(2)}) async-start(), calls=%async_computation.13 | async-start | bytes 2621440 | tf_op jit(solution)/shard_map/all_gather | solution.py:145
  12.6 25.4 %copy-start.21 = (bf16[512,1024]{1,0:T(8,128)(2,1)}, bf16[512,1024]{1,0:T(8,128)(2,1)S(1)}, u32[]{:S(2)}) copy-start(bf16[512,1024]{1,0:T(8,128)(2,1)S(1)} %fusion.33) | copy-start | bytes 3145732
  12.6 24.7 %copy-start.56 = (s32[4]{0:T(128)S(1)}, s32[4]{0:T(128)}, u32[]{:S(2)}) copy-start(s32[4]{0:T(128)} %param.21) | copy-start | bytes 52
  12.6 25.4 %copy-start.45 = (f32[1024]{0:T(1024)S(1)}, f32[1024]{0:T(1024)}, u32[]{:S(2)}) copy-start(f32[1024]{0:T(1024)} %param.23) | copy-start | bytes 12292
  37.2 125.6 %all-gather.12.cloned.1.call-start = ((), (), s32[]{:S(2)}) async-start(), calls=%async_computation.10 | async-start | bytes 2621440 | tf_op jit(solution)/shard_map/all_gather | solution.py:144
  38.0 57.8 %copy-start.16 = (f32[512,64]{0,1:T(8,128)}, f32[512,64]{0,1:T(8,128)S(1)}, u32[]{:S(2)}) copy-start(f32[512,64]{0,1:T(8,128)S(1)} %get-tuple-element.676) | copy-start | bytes 393220
  38.0 57.8 %copy-start.29 = (f32[512,64]{0,1:T(8,128)}, f32[512,64]{0,1:T(8,128)S(1)}, u32[]{:S(2)}) copy-start(f32[512,64]{0,1:T(8,128)S(1)} %get-tuple-element.677) | copy-start | bytes 393220
  38.3 53.8 %copy-start.22 = (bf16[1,1,2,256,1024]{4,3,2,1,0:T(8,128)(2,1)}, bf16[1,1,2,256,1024]{4,3,2,1,0:T(8,128)(2,1)S(1)}, u32[]{:S(2)}) copy-start(bf16[1,1,2,256,1024]{4,3,2,1,0:T(8,128)(2,1)S(1)} %fusion.41) | copy-start | bytes 3145732
  62.3 258.6 %all-gather.20.cloned.1.call-start = ((), (), s32[]{:S(2)}) async-start(), calls=%async_computation.14 | async-start | bytes 2359296 | tf_op jit(solution)/shard_map/all_gather | solution.py:98
  62.9 264.2 %all-gather.22.cloned.1.call-start = ((), (), s32[]{:S(2)}) async-start(), calls=%async_computation.15 | async-start | bytes 10616832 | tf_op jit(solution)/shard_map/all_gather | solution.py:99
  63.6 312.5 %all-gather.24.cloned.1.call-start = ((), (), s32[]{:S(2)}) async-start(), calls=%async_computation.16 | async-start | bytes 10616832 | tf_op jit(solution)/shard_map/all_gather | solution.py:100
  64.4 402.6 %all-gather.26.cloned.1.call-start = ((), (), s32[]{:S(2)}) async-start(), calls=%async_computation.17 | async-start | bytes 10616832 | tf_op jit(solution)/shard_map/all_gather | solution.py:101
  65.1 635.4 %reduce-scatter.10.cloned.1.call-start = ((), (), s32[]{:S(2)}) async-start(), calls=%async_computation.18 | async-start | bytes 2621440 | tf_op jit(solution)/shard_map/reduce_scatter | solution.py:270
  171.1 4.8 copy-start.27
  171.1 4.8 copy-start.31
  171.1 6.1 copy-start
  189.5 5.9 copy-start
  209.0 4.8 copy-start.27
  209.0 4.8 copy-start.31
  209.0 6.0 copy-start
  228.5 4.8 copy-start.27
  228.5 4.8 copy-start.31
  228.5 6.0 copy-start
  248.0 6.0 copy-start
  267.6 5.9 copy-start
  287.0 6.2 copy-start
  306.9 6.0 copy-start
  321.0 4.9 copy-start.49
  485.0 9.2 copy-start.7
  485.0 9.2 copy-start.20
  494.2 8.7 copy-start.37
  666.7 72.8 %reduce-scatter.12.cloned.1.call-start = ((), (), s32[]{:S(2)}) async-start(), calls=%async_computation.19 | async-start | bytes 2621440 | tf_op jit(solution)/shard_map/reduce_scatter | solution.py:273
  670.6 214.4 %reduce-scatter.14.cloned.1.call-start = ((), (), s32[]{:S(2)}) async-start(), calls=%async_computation.20 | async-start | bytes 4325376 | tf_op jit(solution)/shard_map/reduce_scatter | solution.py:300
  679.5 348.0 %reduce-scatter.20.cloned.1.call-start = ((), (), s32[]{:S(2)}) async-start(), calls=%async_computation.23 | async-start | bytes 4325376 | tf_op jit(solution)/shard_map/reduce_scatter | solution.py:303
  684.6 17.3 copy-start.12
  684.6 17.3 copy-start.44
  684.6 17.3 copy-start.54
  684.7 479.5 %reduce-scatter.16.cloned.1.call-start = ((), (), s32[]{:S(2)}) async-start(), calls=%async_computation.21 | async-start | bytes 2162688 | tf_op jit(solution)/shard_map/reduce_scatter | solution.py:301
  705.9 37.2 %copy-start.14 = (bf16[512,1024]{1,0:T(8,128)(2,1)S(1)}, bf16[512,1024]{1,0:T(8,128)(2,1)}, u32[]{:S(2)}) copy-start(bf16[512,1024]{1,0:T(8,128)(2,1)} %multiply_convert_fusion.4) | copy-start | bytes 3145732
  705.9 594.0 %reduce-scatter.18.cloned.1.call-start = ((), (), s32[]{:S(2)}) async-start(), calls=%async_computation.22 | async-start | bytes 2162688 | tf_op jit(solution)/shard_map/reduce_scatter | solution.py:302
  743.0 767.2 %reduce-scatter.22.cloned.1.call-start = ((), (), s32[]{:S(2)}) async-start(), calls=%async_computation.24 | async-start | bytes 19464192 | tf_op jit(solution)/shard_map/reduce_scatter | solution.py:198
  754.6 968.1 %reduce-scatter.24.cloned.1.call-start = ((), (), s32[]{:S(2)}) async-start(), calls=%async_computation.25 | async-start | bytes 19464192 | tf_op jit(solution)/shard_map/reduce_scatter | solution.py:199
  766.3 1168.9 %reduce-scatter.26.cloned.1.call-start = ((), (), s32[]{:S(2)}) async-start(), calls=%async_computation.26 | async-start | bytes 19464192 | tf_op jit(solution)/shard_map/reduce_scatter | solution.py:200
  783.3 9.9 copy-start.19
  783.3 9.9 copy-start.25
  (69 other events, 147.4 us)
Sparse Core Ops, SparseCore 0:
  9.6 24.7 all-gather.15
  36.1 21.7 all-gather.9
  59.5 28.7 all-gather.13
  90.5 34.7 all-gather.17
  127.6 35.1 all-gather.11
  164.2 29.0 all-gather.19
  195.0 90.2 all-gather.21
  286.9 89.1 all-gather.23
  377.8 89.1 all-gather.25
  666.9 33.6 reduce-scatter.9
  704.4 35.1 reduce-scatter.11
  742.3 142.7 reduce-scatter.13
  887.9 139.4 reduce-scatter.19
  1030.1 133.9 reduce-scatter.15
  1166.9 132.9 reduce-scatter.17
  1306.7 203.4 reduce-scatter.21
  1517.1 205.6 reduce-scatter.23
  1729.6 205.6 reduce-scatter.25
where the time goes:
time: 1950 us; the launch traced here: 1940 us
  waiting for transfers between devices  1390 us (71%)
  matrix products  298 us (15%)
  local copies, waits for them, and re-layouts  101 us (5%)
  other arithmetic  95.8 us (5%)
  blocking collectives  40.1 us (2%)
    reduce_scatter x1, waiting for transfers between devices, shards(): lax.psum_scatter(down_wgrad, ('ctx', 'fsdp'), scatter_dimension=0, tiled=...  213 us
    reduce_scatter x1, waiting for transfers between devices, shards(): lax.psum_scatter(up_wgrad, ('ctx', 'fsdp'), scatter_dimension=0, tiled=True)  213 us
    reduce_scatter x1, waiting for transfers between devices, shards(): lax.psum_scatter(gate_wgrad, ('ctx', 'fsdp'), scatter_dimension=0, tiled=...  210 us
    reduce_scatter x1, waiting for transfers between devices, shards(): lax.psum_scatter(output_wgrad, ('ctx', 'fsdp'), scatter_dimension=0, tile...  142 us
    reduce_scatter x1, waiting for transfers between devices, shards(): lax.psum_scatter(key_wgrad, ('ctx', 'fsdp'), scatter_dimension=0, tiled=T...  137 us
    reduce_scatter x1, waiting for transfers between devices, shards(): lax.psum_scatter(value_wgrad, ('ctx', 'fsdp'), scatter_dimension=0, tiled...  136 us
    all_gather x1, waiting for transfers between devices, shards(): lax.all_gather(w_down, 'fsdp', axis=0, tiled=True)  80.4 us
    dot_general x16, matrix products, scores_for(): jnp.einsum('qhgd,khd->qhgk', query_low, key_block.reshape(block_size, KV_...  53.8 us
  transfers between devices with their start and end apart: 18, of which 16 were waited for; matrix products, arithmetic and copies ran while one was open for 14% of the time, Pallas kernels for 0%

commit v1 on v0

--- a/solution.py
+++ b/solution.py
@@ -55,6 +55,76 @@
     return lax.dot_general(
         left, right, (((1,), (1,)), ((), ())), preferred_element_type=jnp.float32
     )
+
+
+def bit_count(size):
+    return size.bit_length() - 1
+
+
+def swap(value, axis_name, bit):
+    size = lax.axis_size(axis_name)
+    return lax.ppermute(value, axis_name, [(i, i ^ (1 << bit)) for i in range(size)])
+
+
+def own_bit(axis_name, bit):
+    return (lax.axis_index(axis_name) >> bit) & 1
+
+
+def ctx_bits(flip):
+    bits = list(range(bit_count(lax.axis_size("ctx"))))
+    return bits[::-1] if flip else bits
+
+
+def scatter_sum(value, flip, with_fsdp=True):
+    ctx_n = bit_count(lax.axis_size("ctx"))
+    fsdp_n = bit_count(lax.axis_size("fsdp")) if with_fsdp else 0
+    names = [("ctx", b) for b in range(ctx_n - 1, -1, -1)]
+    names += [("fsdp", b) for b in range(fsdp_n - 1, -1, -1)]
+    steps = [("fsdp", 0)] if with_fsdp else []
+    steps += [("ctx", b) for b in ctx_bits(flip)]
+    steps += [("fsdp", b) for b in range(1, fsdp_n)]
+    rows = value.shape[0] >> len(names)
+    value = value.reshape([2] * len(names) + [rows, value.shape[1]])
+    for count, step in enumerate(steps):
+        axis = names.index(step)
+        names.pop(axis)
+        mine = own_bit(*step)
+        gone = lax.dynamic_index_in_dim(value, 1 - mine, axis, keepdims=False)
+        kept = lax.dynamic_index_in_dim(value, mine, axis, keepdims=False)
+        got = swap(gone.reshape(-1, gone.shape[-1]), *step).reshape(kept.shape)
+        value = kept.astype(jnp.float32) + got.astype(jnp.float32)
+        if count + 1 < len(steps):
+            value = value.astype(jnp.bfloat16)
+    return value
+
+
+def gather_rows(shard, flip):
+    ctx_size, fsdp_size = lax.axis_size("ctx"), lax.axis_size("fsdp")
+    ctx_n, fsdp_n = bit_count(ctx_size), bit_count(fsdp_size)
+    rows = shard.shape[0] // ctx_size
+    cols = shard.shape[1]
+    order = [("fsdp", b) for b in range(fsdp_n - 1, -1, -1)]
+    order += [("ctx", b) for b in range(ctx_n - 1, -1, -1)]
+    steps = [("fsdp", b) for b in range(fsdp_n - 1, 0, -1)]
+    steps += [("ctx", b) for b in ctx_bits(flip)] + [("fsdp", 0)]
+    value = lax.dynamic_slice_in_dim(shard, lax.axis_index("ctx") * rows, rows)
+    names = []
+    for step in steps:
+        got = swap(value.reshape(-1, cols), *step).reshape(value.shape)
+        low = own_bit(*step) == 0
+        axis = sum(order.index(n) < order.index(step) for n in names)
+        names.insert(axis, step)
+        value = jnp.stack(
+            [jnp.where(low, value, got), jnp.where(low, got, value)], axis=axis
+        )
+    return value.reshape(-1, cols)
+
+
+def sum_all(value):
+    for axis_name in ("fsdp", "ctx"):
+        for bit in range(bit_count(lax.axis_size(axis_name))):
+            value = value + swap(value, axis_name, bit)
+    return value
 
 
 def shards(
@@ -92,13 +162,17 @@
     cosine, sine_part = angles(own_pos, HEAD_DIM)
     inputs_now = tokens.reshape(local_rows, model_width).astype(jnp.float32)
     full_query, full_key, full_value, full_output, full_gate, full_up, full_down = (
-        lax.all_gather(w_query, "fsdp", axis=0, tiled=True),
-        lax.all_gather(w_key, "fsdp", axis=0, tiled=True),
-        lax.all_gather(w_value, "fsdp", axis=0, tiled=True),
-        lax.all_gather(w_output, "fsdp", axis=0, tiled=True),
-        lax.all_gather(w_gate, "fsdp", axis=0, tiled=True),
-        lax.all_gather(w_up, "fsdp", axis=0, tiled=True),
-        lax.all_gather(w_down, "fsdp", axis=0, tiled=True),
+        gather_rows(w_query, False),
+        gather_rows(w_key, True),
+        gather_rows(w_value, True),
+        gather_rows(w_output, True),
+        gather_rows(w_gate, False),
+        gather_rows(w_up, True),
+        None,
+    )
+    middle = w_down.shape[1] // 2
+    full_down = jnp.concatenate(
+        [gather_rows(w_down[:, :middle], False), gather_rows(w_down[:, middle:], True)], axis=1
     )
     attn_out, attn_normal, attn_factor = norm_parts(inputs_now, attn_gain)
     attn_in = attn_out.astype(jnp.bfloat16)
@@ -141,8 +215,10 @@
         jnp.zeros((local_rows, KV_HEADS, group_size), jnp.float32),
         jnp.zeros((local_rows, KV_HEADS, group_size, HEAD_DIM), jnp.float32),
     )
-    key_rows = lax.all_gather(key_low, "ctx", axis=0, tiled=True)
-    value_rows = lax.all_gather(value_low, "ctx", axis=0, tiled=True)
+    both_rows = lax.all_gather(
+        jnp.concatenate([key_low, value_low], axis=1), "ctx", axis=0, tiled=True
+    )
+    key_rows, value_rows = jnp.split(both_rows, 2, axis=1)
     block_size = math.gcd(key_rows.shape[0], 256)
 
     def forward_advance(block_index, running_now):
@@ -182,26 +258,26 @@
     result = residual + jnp.dot(activation, full_down, preferred_element_type=jnp.float32)
     output = result.astype(jnp.bfloat16).reshape(tokens.shape)
     grad_low = cotangent.reshape(local_rows, model_width)
-    down_wgrad = contract_rows(activation, grad_low)
+    down_wgrad = contract_rows(activation, grad_low).astype(jnp.bfloat16)
     act_grad = times_transposed(grad_low, full_down)
     gate_grad = (
         act_grad * up_value * gate_sigmoid * (1.0 + gate_value * (1.0 - gate_sigmoid))
     ).astype(jnp.bfloat16)
     up_grad = (act_grad * gate_silu).astype(jnp.bfloat16)
-    gate_wgrad = contract_rows(ffn_in, gate_grad)
-    up_wgrad = contract_rows(ffn_in, up_grad)
+    gate_wgrad = contract_rows(ffn_in, gate_grad).astype(jnp.bfloat16)
+    up_wgrad = contract_rows(ffn_in, up_grad).astype(jnp.bfloat16)
     ffn_in_grad = times_transposed(gate_grad, full_gate) + times_transposed(up_grad, full_up)
     ffn_back, ffn_gain_part = norm_back(ffn_in_grad, ffn_normal, ffn_factor, ffn_gain)
     ffn_gain_wgrad = jnp.sum(ffn_gain_part, axis=0)
     residual_grad = grad_low.astype(jnp.float32) + ffn_back
-    gate_sum, up_sum, down_sum, ffn_gain_sum = (
-        lax.psum_scatter(gate_wgrad, ("ctx", "fsdp"), scatter_dimension=0, tiled=True),
-        lax.psum_scatter(up_wgrad, ("ctx", "fsdp"), scatter_dimension=0, tiled=True),
-        lax.psum_scatter(down_wgrad, ("ctx", "fsdp"), scatter_dimension=0, tiled=True),
-        lax.psum_scatter(ffn_gain_wgrad, ("ctx", "fsdp"), scatter_dimension=0, tiled=True),
+    gate_sum = scatter_sum(gate_wgrad, False)
+    up_sum = scatter_sum(up_wgrad, True)
+    down_sum = jnp.concatenate(
+        [scatter_sum(down_wgrad[:, :middle], False), scatter_sum(down_wgrad[:, middle:], True)],
+        axis=1,
     )
     residual_low = residual_grad.astype(jnp.bfloat16)
-    output_wgrad = contract_rows(mixed_low, residual_low)
+    output_wgrad = contract_rows(mixed_low, residual_low).astype(jnp.bfloat16)
     mixed_grad = times_transposed(residual_low, full_output).astype(jnp.bfloat16)
     mixed_grad = mixed_grad.reshape(local_rows, KV_HEADS, group_size, HEAD_DIM)
     row_delta = jnp.sum(mixed_grad.astype(jnp.float32) * attn_mix, axis=-1)
@@ -210,8 +286,7 @@
         jnp.zeros((seq_rows, KV_HEADS * HEAD_DIM), jnp.float32),
         jnp.zeros((seq_rows, KV_HEADS * HEAD_DIM), jnp.float32),
     )
-    backward_key_rows = lax.all_gather(key_low, "ctx", axis=0, tiled=True)
-    backward_value_rows = lax.all_gather(value_low, "ctx", axis=0, tiled=True)
+    backward_key_rows, backward_value_rows = key_rows, value_rows
     backward_block_size = math.gcd(backward_key_rows.shape[0], 256)
 
     def backward_advance(block_index, running_now):
@@ -266,14 +341,8 @@
     query_grad, key_grad_all, value_grad_all = lax.fori_loop(
         0, backward_key_rows.shape[0] // backward_block_size, backward_advance, back_state
     )
-    key_grad, value_grad = (
-        lax.psum_scatter(
-            key_grad_all.astype(jnp.bfloat16), "ctx", scatter_dimension=0, tiled=True
-        ).astype(jnp.float32),
-        lax.psum_scatter(
-            value_grad_all.astype(jnp.bfloat16), "ctx", scatter_dimension=0, tiled=True
-        ).astype(jnp.float32),
-    )
+    key_grad = scatter_sum(key_grad_all.astype(jnp.bfloat16), False, False)
+    value_grad = scatter_sum(value_grad_all.astype(jnp.bfloat16), True, False)
     key_grad = key_grad.reshape(local_rows, KV_HEADS, HEAD_DIM)
     key_turned = key_grad * cosine + turn_back(key_grad * sine_part)
     key_back, key_gain_part = norm_back(key_turned, key_normal, key_factor, key_gain)
@@ -285,9 +354,10 @@
     query_gain_local = jnp.sum(query_gain_part, axis=(0, 1))
     query_raw_grad = query_back.reshape(local_rows, Q_HEADS * HEAD_DIM).astype(jnp.bfloat16)
     value_raw_grad = value_grad.astype(jnp.bfloat16)
-    query_wgrad = contract_rows(attn_in, query_raw_grad)
-    key_wgrad = contract_rows(attn_in, key_raw_grad)
-    value_wgrad = contract_rows(attn_in, value_raw_grad)
+    query_wgrad = contract_rows(attn_in, query_raw_grad).astype(jnp.bfloat16)
+    pair_wgrad = contract_rows(
+        attn_in, jnp.concatenate([key_raw_grad, value_raw_grad], axis=1)
+    ).astype(jnp.bfloat16)
     attn_in_grad = (
         times_transposed(query_raw_grad, full_query)
         + times_transposed(key_raw_grad, full_key)
@@ -296,14 +366,18 @@
     attn_back, attn_gain_part = norm_back(attn_in_grad, attn_normal, attn_factor, attn_gain)
     attn_gain_wgrad = jnp.sum(attn_gain_part, axis=0)
     input_grad = (residual_grad + attn_back).reshape(tokens.shape)
-    query_sum, key_sum, value_sum, output_sum, attn_gain_sum = (
-        lax.psum_scatter(query_wgrad, ("ctx", "fsdp"), scatter_dimension=0, tiled=True),
-        lax.psum_scatter(key_wgrad, ("ctx", "fsdp"), scatter_dimension=0, tiled=True),
-        lax.psum_scatter(value_wgrad, ("ctx", "fsdp"), scatter_dimension=0, tiled=True),
-        lax.psum_scatter(output_wgrad, ("ctx", "fsdp"), scatter_dimension=0, tiled=True),
-        lax.psum_scatter(attn_gain_wgrad, ("ctx", "fsdp"), scatter_dimension=0, tiled=True),
-    )
-    query_gain_sum, key_gain_sum = lax.psum((query_gain_local, key_gain_local), ("ctx", "fsdp"))
+    query_sum = scatter_sum(query_wgrad, False)
+    pair_sum = scatter_sum(pair_wgrad, True)
+    key_sum, value_sum = jnp.split(pair_sum, 2, axis=1)
+    output_sum = scatter_sum(output_wgrad, True)
+    gains = sum_all(
+        jnp.concatenate([attn_gain_wgrad, ffn_gain_wgrad, query_gain_local, key_gain_local])
+    )
+    share = model_width // (ctx_count * lax.axis_size("fsdp"))
+    first = (ctx_rank * lax.axis_size("fsdp") + lax.axis_index("fsdp")) * share
+    attn_gain_sum = lax.dynamic_slice_in_dim(gains, first, share)
+    ffn_gain_sum = lax.dynamic_slice_in_dim(gains, model_width + first, share)
+    query_gain_sum, key_gain_sum = jnp.split(gains[2 * model_width :], 2)
     return (
         output,
         input_grad,

time: 1950 us -> 1190 us (0.61)
  waiting for transfers between devices: 1390 us -> 333 us
  local copies, waits for them, and re-layouts: 101 us -> 234 us
  other arithmetic: 95.8 us -> 182 us
  starting transfers between devices: 1.83 us -> 85.7 us
  blocking collectives: 40.1 us -> 0 us
  matrix products: 298 us -> 321 us
    reduce_scatter x9 -> x0, waiting for transfers between devices: 1140 us -> none  [the longest x1 213 us: shards(): lax.psum_scatter(down_wgrad, ('ctx', 'fsdp'), scatter_dimension=0, tiled=...]
    ppermute x0 -> x84, waiting for transfers between devices: none -> 333 us  [swap(): lax.ppermute(value, axis_name, [(i, i ^ 1 << bit) for i in range(size)])]
    all_gather x9 -> x1, waiting for transfers between devices: 242 us -> 0.01 us  [shards(): lax.all_gather(jnp.concatenate([key_low, value_low], axis=1), 'ctx', axis...]
    ppermute x0 -> x84, starting transfers between devices: none -> 85.7 us  [swap(): lax.ppermute(value, axis_name, [(i, i ^ 1 << bit) for i in range(size)])]
    dynamic_slice x8 -> x57, local copies, waits for them, and re-layouts: 7.8 us -> 60.5 us  [the longest x16 31.3 us: backward_advance(): lax.dynamic_slice_in_dim(key_grad_all, offset, backward_block_size)]
    unnamed x1 -> x0, blocking collectives: 40.1 us -> none
    another operation x2 -> x30, local copies, waits for them, and re-layouts: 4.97 us -> 44.9 us  [the longest x28 39.9 us: gather_rows(): jnp.stack([jnp.where(low, value, got), jnp.where(low, got, value)], axis=...]
    select_n x0 -> x32, other arithmetic: none -> 32 us  [gather_rows(): jnp.where(low, value, got)]
  transfers between devices with their start and end apart: 18 -> 85, of which waited for: 16 -> 37; matrix products, arithmetic and copies ran while one was open for 14% -> 27% of each run, Pallas kernels for 0% -> 0%
where the time goes in v1:
time: 1190 us; the launch traced here: 1180 us
  waiting for transfers between devices  333 us (28%)
  matrix products  321 us (27%)
  local copies, waits for them, and re-layouts  234 us (20%)
  other arithmetic  182 us (15%)
  starting transfers between devices  85.7 us (7%)
  between operations  17.3 us (1%)
    ppermute x84, waiting for transfers between devices, swap(): lax.ppermute(value, axis_name, [(i, i ^ 1 << bit) for i in range(size)])  333 us
    ppermute x84, starting transfers between devices, swap(): lax.ppermute(value, axis_name, [(i, i ^ 1 << bit) for i in range(size)])  85.7 us
    dot_general x16, matrix products, scores_for(): jnp.einsum('qhgd,khd->qhgk', query_low, key_block.reshape(block_size, KV_...  47.9 us
    dot_general x8, matrix products, backward_advance(): jnp.einsum('qhgk,qhgd->khd', attn_probs.astype(jnp.bfloat16), mixed_grad,...  45 us
    dot_general x7, matrix products, times_transposed(): lax.dot_general(left, right, (((1,), (1,)), ((), ())), preferred_element_...  42.8 us
    another operation x28, local copies, waits for them, and re-layouts, gather_rows(): jnp.stack([jnp.where(low, value, got), jnp.where(low, got, value)], axis=...  39.9 us
    reduce_sum x8, other arithmetic, forward_advance(): denom_sum = denom_sum * shrink + jnp.sum(attn_probs, axis=-1)  37 us
    dot_general x8, matrix products, forward_advance(): jnp.einsum('qhgk,khd->qhgd', attn_probs.astype(jnp.bfloat16), value_block...  35.1 us
  transfers between devices with their start and end apart: 85, of which 37 were waited for; matrix products, arithmetic and copies ran while one was open for 27% of the time, Pallas kernels for 0%

profile of v1, /device:TPU:0, one launch (start us, length us, event | category | flops | bytes accessed | tf_op | source)
XLA Modules:
  0.0 1176.2 jit_solution(1562967875246539860)
XLA Ops:
  49.8 13.0 %collective-permute-done.1 = bf16[64,512]{1,0:T(8,128)(2,1)S(1)} collective-permute-done((bf16[64,512]{1,0:T(8,128)(2,1)S(1)}, bf16[64,512]{1,0:T(8,128)(2,1)S(1)}, u32[]{:S(2)}, u32[]{:S(2)}) %collective-permute-start.1) | collective-permute-done | bytes 65568 | tf_op jit(solution)/shard_map/ppermute | solution.py:66
  93.4 7.3 collective-permute-done.21
  154.5 32.8 %collective-permute-done.38 = bf16[1152,512]{1,0:T(8,128)(2,1)} collective-permute-done((bf16[1152,512]{1,0:T(8,128)(2,1)}, bf16[1152,512]{1,0:T(8,128)(2,1)}, u32[]{:S(2)}, u32[]{:S(2)}) %collective-permute-start.38) | collective-permute-done | bytes 1179680 | tf_op jit(solution)/shard_map/ppermute | solution.py:66
  194.4 56.2 %collective-permute-done.23 = bf16[256,4608]{1,0:T(8,128)(2,1)S(1)} collective-permute-done((bf16[256,4608]{1,0:T(8,128)(2,1)S(1)}, bf16[256,4608]{1,0:T(8,128)(2,1)S(1)}, u32[]{:S(2)}, u32[]{:S(2)}) %collective-permute-start.23) | collective-permute-done | bytes 2359328 | tf_op jit(solution)/shard_map/ppermute | solution.py:66
  272.3 4.9 fusion.128
  277.2 131.4 %while.36 = (s32[]{:T(128)}, f32[512,8,2]{0,2,1:T(2,128)S(1)}, f32[512,8,2]{0,2,1:T(2,128)S(1)}, f32[512,8,2,64]{0,3,2,1:T(8,128)}, s32[2048]{0:T(1024)S(1)}, /*...) while((s32[]{:T(128)}, f32[512,8,2]{0,2,1:T(2,128)S(1)}, ...), condition=%wide.region_6.7_spmd.clone, body=%wide.region_3.6_spmd.clone.sunk | while | flops 566140928 | bytes 66595060 | solution.py:244
  415.3 6.2 broadcast_select_fusion.4
  421.5 8.2 pad_maximum_fusion
  429.7 8.5 copy.263
  438.2 7.2 broadcast_select_fusion.2
  445.4 8.3 pad_maximum_fusion.1
  453.7 8.4 copy.279
  462.1 11.3 fusion.136
  473.3 7.5 fusion.137
  480.8 16.2 %fusion.31 = (bf16[512,4608]{1,0:T(8,128)(2,1)}, bf16[512,4608]{1,0:T(8,128)(2,1)}, bf16[512,4608]{1,0:T(8,128)(2,1)}) fusion(f32[512,4608]{1,0:T(8,128)} %fusion.136, f32[512,4608]{1,0:T(8,128)} %fusion.137, bf16[512,1024]{1,0:T(8,128)(2,1)S(1)} %bitcast.869, bf16[4608,512]{1,0:T(8,128)(2,1)} %bitcast.800, bf16[4608,512]{1,0:T(8,128)(2,1)} %bitcast.804), kind=kOutput, calls=%fused_computation.60 | convolution fusion | flops 4886102016 | bytes 43515904 | tf_op jit(solution)/shard_map/dot_general | solution.py:55
  497.1 9.2 fusion.138
  506.3 8.6 multiply_reduce_fusion.1
  521.5 7.7 convolution_convert_fusion.1
  529.2 7.5 convolution_convert_fusion.2
  536.8 8.5 add_convert_fusion
  545.4 7.6 convolution_convert_fusion
  561.3 263.5 %while.37 = (s32[]{:T(128)}, f32[512,8,2,64]{0,3,2,1:T(8,128)S(1)}, f32[2048,512]{1,0:T(8,128)}, f32[2048,512]{0,1:T(8,128)}, bf16[2048,512]{0,1:T(8,128)(2,1)},...) while((s32[]{:T(128)}, f32[512,8,2,64]{0,3,2,1:T(8,128)S(1)}, ...), condition=%wide.region_11.12_spmd.clone, body=%wide.region_10.11_spmd.clone.sunk | while | flops 1369702400 | bytes 97102248 | solution.py:341
  587.1 5.6 fusion.234
  620.0 5.6 fusion.234
  652.8 5.6 fusion.234
  685.8 5.6 fusion.234
  718.7 5.6 fusion.234
  751.5 5.6 fusion.234
  784.5 5.6 fusion.234
  817.3 5.6 fusion.234
  856.2 6.7 constant_dynamic-slice_fusion.21
  878.8 7.7 collective-permute-done.41
  906.4 7.0 collective-permute-start.46
  949.2 31.4 %collective-permute-done.55 = bf16[256,1024]{1,0:T(8,128)(2,1)S(1)} collective-permute-done((bf16[256,1024]{1,0:T(8,128)(2,1)S(1)}, bf16[256,1024]{1,0:T(8,128)(2,1)S(1)}, u32[]{:S(2)}, u32[]{:S(2)}) %collective-permute-start.55) | collective-permute-done | bytes 524320 | tf_op jit(solution)/shard_map/ppermute | solution.py:66
  981.6 9.3 collective-permute-done.60
  991.9 20.5 %collective-permute-done.56 = bf16[128,1024]{1,0:T(8,128)(2,1)S(1)} collective-permute-done((bf16[128,1024]{1,0:T(8,128)(2,1)S(1)}, bf16[128,1024]{1,0:T(8,128)(2,1)S(1)}, u32[]{:S(2)}, u32[]{:S(2)}) %collective-permute-start.56) | collective-permute-done | bytes 262176 | tf_op jit(solution)/shard_map/ppermute | solution.py:66
  1013.2 5.6 collective-permute-done.61
  1019.0 5.3 collective-permute-done.57
  1024.6 5.8 collective-permute-done.62
  1039.3 6.0 collective-permute-done.81
  1045.5 6.4 fusion.26
  1056.3 5.0 collective-permute-done.82
  1072.1 24.6 %collective-permute-done.65 = bf16[256,4608]{1,0:T(8,128)(2,1)S(1)} collective-permute-done((bf16[256,4608]{1,0:T(8,128)(2,1)S(1)}, bf16[256,4608]{1,0:T(8,128)(2,1)S(1)}, u32[]{:S(2)}, u32[]{:S(2)}) %collective-permute-start.65) | collective-permute-done | bytes 2359328 | tf_op jit(solution)/shard_map/ppermute | solution.py:66
  1098.2 20.8 %collective-permute-done.70 = bf16[256,4608]{1,0:T(8,128)(2,1)S(1)} collective-permute-done((bf16[256,4608]{1,0:T(8,128)(2,1)S(1)}, bf16[256,4608]{1,0:T(8,128)(2,1)S(1)}, u32[]{:S(2)}, u32[]{:S(2)}) %collective-permute-start.70) | collective-permute-done | bytes 2359328 | tf_op jit(solution)/shard_map/ppermute | solution.py:66
  1121.1 10.6 collective-permute-done.66
  1138.0 7.3 collective-permute-done.67
  1148.4 8.5 collective-permute-done.72
  1159.8 8.2 collective-permute-done.73
  (1010 shorter events, 670.3 us)
Async XLA Ops:
  7.2 265.1 %all-gather.2.cloned.1.call-start = ((), (), s32[]{:S(2)}) async-start(), calls=%async_computation | async-start | bytes 5242880 | tf_op jit(solution)/shard_map/all_gather | solution.py:218
  8.0 26.0 %collective-permute-start.5 = (bf16[32,512]{1,0:T(8,128)(2,1)S(1)}, bf16[32,512]{1,0:T(8,128)(2,1)S(1)}, u32[]{:S(2)}, u32[]{:S(2)}) collective-permute-start(bf16[32,512]{1,0:T(8,128)(2,1)S(1)} %constant_dynamic-slice_fusion.42), channel_id=1, source_target_pairs={{0,4},{1,5},{2,6},{3,7},{4,0},{5,1},{6,2},{7,3},{8,12},{9,13},{10,... | collective-permute-start | bytes 98312 | tf_op jit(solution)/shard_map/ppermute | solution.py:66
  12.8 22.1 %collective-permute-start = (bf16[32,512]{1,0:T(8,128)(2,1)S(1)}, bf16[32,512]{1,0:T(8,128)(2,1)S(1)}, u32[]{:S(2)}, u32[]{:S(2)}) collective-permute-start(bf16[32,512]{1,0:T(8,128)(2,1)S(1)} %constant_dynamic-slice_fusion.43), channel_id=1, source_target_pairs={{0,4},{1,5},{2,6},{3,7},{4,0},{5,1},{6,2},{7,3},{8,12},{9,13},{10,... | collective-permute-start | bytes 98312 | tf_op jit(solution)/shard_map/ppermute | solution.py:66
  13.6 25.0 %collective-permute-start.10 = (bf16[32,1024]{1,0:T(8,128)(2,1)S(1)}, bf16[32,1024]{1,0:T(8,128)(2,1)S(1)}, u32[]{:S(2)}, u32[]{:S(2)}) collective-permute-start(bf16[32,1024]{1,0:T(8,128)(2,1)S(1)} %constant_dynamic-slice_fusion.41), channel_id=1, source_target_pairs={{0,4},{1,5},{2,6},{3,7},{4,0},{5,1},{6,2},{7,3},{8,12},{9,13},{10,... | collective-permute-start | bytes 196616 | tf_op jit(solution)/shard_map/ppermute | solution.py:66
  17.4 22.3 %collective-permute-start.15 = (bf16[32,1024]{1,0:T(8,128)(2,1)S(1)}, bf16[32,1024]{1,0:T(8,128)(2,1)S(1)}, u32[]{:S(2)}, u32[]{:S(2)}) collective-permute-start(bf16[32,1024]{1,0:T(8,128)(2,1)S(1)} %constant_dynamic-slice_fusion.40), channel_id=1, source_target_pairs={{0,4},{1,5},{2,6},{3,7},{4,0},{5,1},{6,2},{7,3},{8,12},{9,13},{10,... | collective-permute-start | bytes 196616 | tf_op jit(solution)/shard_map/ppermute | solution.py:66
  19.1 57.0 %collective-permute-start.20 = (bf16[32,4608]{1,0:T(8,128)(2,1)}, bf16[32,4608]{1,0:T(8,128)(2,1)}, u32[]{:S(2)}, u32[]{:S(2)}) collective-permute-start(bf16[32,4608]{1,0:T(8,128)(2,1)} %constant_dynamic-slice_fusion.39), channel_id=1, source_target_pairs={{0,4},{1,5},{2,6},{3,7},{4,0},{5,1},{6,2},{7,3},{8,12},{9,13},{10,... | collective-permute-start | bytes 884744 | tf_op jit(solution)/shard_map/ppermute | solution.py:66
  34.0 44.9 %collective-permute-start.25 = (bf16[32,4608]{1,0:T(8,128)(2,1)}, bf16[32,4608]{1,0:T(8,128)(2,1)S(1)}, u32[]{:S(2)}, u32[]{:S(2)}) collective-permute-start(bf16[32,4608]{1,0:T(8,128)(2,1)} %constant_dynamic-slice_fusion.38), channel_id=1, source_target_pairs={{0,4},{1,5},{2,6},{3,7},{4,0},{5,1},{6,2},{7,3},{8,12},{9,13},{10,... | collective-permute-start | bytes 884744 | tf_op jit(solution)/shard_map/ppermute | solution.py:66
  34.9 27.9 %collective-permute-start.35 = (bf16[144,512]{1,0:T(8,128)(2,1)S(1)}, bf16[144,512]{1,0:T(8,128)(2,1)S(1)}, u32[]{:S(2)}, u32[]{:S(2)}) collective-permute-start(bf16[144,512]{1,0:T(8,128)(2,1)S(1)} %constant_dynamic-slice_fusion.36), channel_id=1, source_target_pairs={{0,4},{1,5},{2,6},{3,7},{4,0},{5,1},{6,2},{7,3},{8,12},{9,13},{10,... | collective-permute-start | bytes 442376 | tf_op jit(solution)/shard_map/ppermute | solution.py:66
  38.6 26.4 %collective-permute-start.30 = (bf16[144,512]{1,0:T(8,128)(2,1)S(1)}, bf16[144,512]{1,0:T(8,128)(2,1)S(1)}, u32[]{:S(2)}, u32[]{:S(2)}) collective-permute-start(bf16[144,512]{1,0:T(8,128)(2,1)S(1)} %constant_dynamic-slice_fusion.37), channel_id=1, source_target_pairs={{0,4},{1,5},{2,6},{3,7},{4,0},{5,1},{6,2},{7,3},{8,12},{9,13},{10,... | collective-permute-start | bytes 442376 | tf_op jit(solution)/shard_map/ppermute | solution.py:66
  47.3 15.5 %collective-permute-start.1 = (bf16[64,512]{1,0:T(8,128)(2,1)S(1)}, bf16[64,512]{1,0:T(8,128)(2,1)S(1)}, u32[]{:S(2)}, u32[]{:S(2)}) collective-permute-start(bf16[64,512]{1,0:T(8,128)(2,1)S(1)} %bitcast.936), channel_id=1, source_target_pairs={{0,2},{1,3},{2,0},{3,1},{4,6},{5,7},{6,4},{7,5},{8,10},{9,11},{10,... | collective-permute-start | bytes 196616 | tf_op jit(solution)/shard_map/ppermute | solution.py:66
  84.4 16.3 %collective-permute-start.21 = (bf16[64,4608]{1,0:T(8,128)(2,1)S(1)}, bf16[64,4608]{1,0:T(8,128)(2,1)S(1)}, u32[]{:S(2)}, u32[]{:S(2)}) collective-permute-start(bf16[64,4608]{1,0:T(8,128)(2,1)S(1)} %bitcast.875), channel_id=1, source_target_pairs={{0,2},{1,3},{2,0},{3,1},{4,6},{5,7},{6,4},{7,5},{8,10},{9,11},{10,... | collective-permute-start | bytes 1769480 | tf_op jit(solution)/shard_map/ppermute | solution.py:66
  85.5 21.6 %collective-permute-start.26 = (bf16[64,4608]{1,0:T(8,128)(2,1)S(1)}, bf16[64,4608]{1,0:T(8,128)(2,1)S(1)}, u32[]{:S(2)}, u32[]{:S(2)}) collective-permute-start(bf16[64,4608]{1,0:T(8,128)(2,1)S(1)} %bitcast.876), channel_id=1, source_target_pairs={{0,2},{1,3},{2,0},{3,1},{4,6},{5,7},{6,4},{7,5},{8,10},{9,11},{10,... | collective-permute-start | bytes 1769480 | tf_op jit(solution)/shard_map/ppermute | solution.py:66
  87.8 36.0 %collective-permute-start.37 = (bf16[576,512]{1,0:T(8,128)(2,1)}, bf16[576,512]{1,0:T(8,128)(2,1)}, u32[]{:S(2)}, u32[]{:S(2)}) collective-permute-start(bf16[576,512]{1,0:T(8,128)(2,1)} %bitcast.180), channel_id=1, source_target_pairs={{0,16},{8,24},{16,0},{24,8},{1,17},{9,25},{17,1},{25,9},{2,18},{10... | collective-permute-start | bytes 1769480 | tf_op jit(solution)/shard_map/ppermute | solution.py:66
  89.6 37.4 %collective-permute-start.32 = (bf16[576,512]{1,0:T(8,128)(2,1)}, bf16[576,512]{1,0:T(8,128)(2,1)}, u32[]{:S(2)}, u32[]{:S(2)}) collective-permute-start(bf16[576,512]{1,0:T(8,128)(2,1)} %bitcast.157), channel_id=1, source_target_pairs={{0,8},{8,0},{16,24},{24,16},{1,9},{9,1},{17,25},{25,17},{2,10},{10... | collective-permute-start | bytes 1769480 | tf_op jit(solution)/shard_map/ppermute | solution.py:66
  92.8 15.6 %collective-permute-start.13 = (bf16[256,1024]{1,0:T(8,128)(2,1)S(1)}, bf16[256,1024]{1,0:T(8,128)(2,1)S(1)}, u32[]{:S(2)}, u32[]{:S(2)}) collective-permute-start(bf16[256,1024]{1,0:T(8,128)(2,1)S(1)} %bitcast.892), channel_id=1, source_target_pairs={{0,16},{8,24},{16,0},{24,8},{1,17},{9,25},{17,1},{25,9},{2,18},{10... | collective-permute-start | bytes 1572872 | tf_op jit(solution)/shard_map/ppermute | solution.py:66
  112.1 36.2 %collective-permute-start.22 = (bf16[128,4608]{1,0:T(8,128)(2,1)}, bf16[128,4608]{1,0:T(8,128)(2,1)}, u32[]{:S(2)}, u32[]{:S(2)}) collective-permute-start(bf16[128,4608]{1,0:T(8,128)(2,1)} %bitcast.113), channel_id=1, source_target_pairs={{0,8},{8,0},{16,24},{24,16},{1,9},{9,1},{17,25},{25,17},{2,10},{10... | collective-permute-start | bytes 3538952 | tf_op jit(solution)/shard_map/ppermute | solution.py:66
  114.0 37.4 %collective-permute-start.27 = (bf16[128,4608]{1,0:T(8,128)(2,1)}, bf16[128,4608]{1,0:T(8,128)(2,1)}, u32[]{:S(2)}, u32[]{:S(2)}) collective-permute-start(bf16[128,4608]{1,0:T(8,128)(2,1)} %bitcast.136), channel_id=1, source_target_pairs={{0,16},{8,24},{16,0},{24,8},{1,17},{9,25},{17,1},{25,9},{2,18},{10... | collective-permute-start | bytes 3538952 | tf_op jit(solution)/shard_map/ppermute | solution.py:66
  123.8 18.5 %collective-permute-start.19 = (bf16[512,1024]{1,0:T(8,128)(2,1)}, bf16[512,1024]{1,0:T(8,128)(2,1)}, u32[]{:S(2)}, u32[]{:S(2)}) collective-permute-start(bf16[512,1024]{1,0:T(8,128)(2,1)} %bitcast.867), channel_id=1, source_target_pairs={{0,1},{1,0},{2,3},{3,2},{4,5},{5,4},{6,7},{7,6},{8,9},{9,8},{10,11... | collective-permute-start | bytes 3145736 | tf_op jit(solution)/shard_map/ppermute | solution.py:66
  126.9 60.3 %collective-permute-start.38 = (bf16[1152,512]{1,0:T(8,128)(2,1)}, bf16[1152,512]{1,0:T(8,128)(2,1)}, u32[]{:S(2)}, u32[]{:S(2)}) collective-permute-start(bf16[1152,512]{1,0:T(8,128)(2,1)} %bitcast.185), channel_id=1, source_target_pairs={{0,8},{8,0},{16,24},{24,16},{1,9},{9,1},{17,25},{25,17},{2,10},{10... | collective-permute-start | bytes 3538952 | tf_op jit(solution)/shard_map/ppermute | solution.py:66
  130.4 60.8 %collective-permute-start.33 = (bf16[1152,512]{1,0:T(8,128)(2,1)}, bf16[1152,512]{1,0:T(8,128)(2,1)}, u32[]{:S(2)}, u32[]{:S(2)}) collective-permute-start(bf16[1152,512]{1,0:T(8,128)(2,1)} %bitcast.161), channel_id=1, source_target_pairs={{0,16},{8,24},{16,0},{24,8},{1,17},{9,25},{17,1},{25,9},{2,18},{10... | collective-permute-start | bytes 3538952 | tf_op jit(solution)/shard_map/ppermute | solution.py:66
  150.6 100.0 %collective-permute-start.23 = (bf16[256,4608]{1,0:T(8,128)(2,1)S(1)}, bf16[256,4608]{1,0:T(8,128)(2,1)S(1)}, u32[]{:S(2)}, u32[]{:S(2)}) collective-permute-start(bf16[256,4608]{1,0:T(8,128)(2,1)S(1)} %bitcast.825), channel_id=1, source_target_pairs={{0,16},{8,24},{16,0},{24,8},{1,17},{9,25},{17,1},{25,9},{2,18},{10... | collective-permute-start | bytes 7077896 | tf_op jit(solution)/shard_map/ppermute | solution.py:66
  153.2 102.2 %collective-permute-start.28 = (bf16[256,4608]{1,0:T(8,128)(2,1)S(1)}, bf16[256,4608]{1,0:T(8,128)(2,1)}, u32[]{:S(2)}, u32[]{:S(2)}) collective-permute-start(bf16[256,4608]{1,0:T(8,128)(2,1)S(1)} %bitcast.824), channel_id=1, source_target_pairs={{0,8},{8,0},{16,24},{24,16},{1,9},{9,1},{17,25},{25,17},{2,10},{10... | collective-permute-start | bytes 7077896 | tf_op jit(solution)/shard_map/ppermute | solution.py:66
  189.1 73.5 %collective-permute-start.39 = (bf16[2304,512]{1,0:T(8,128)(2,1)S(1)}, bf16[2304,512]{1,0:T(8,128)(2,1)}, u32[]{:S(2)}, u32[]{:S(2)}) collective-permute-start(bf16[2304,512]{1,0:T(8,128)(2,1)S(1)} %bitcast.823), channel_id=1, source_target_pairs={{0,1},{1,0},{2,3},{3,2},{4,5},{5,4},{6,7},{7,6},{8,9},{9,8},{10,11... | collective-permute-start | bytes 7077896 | tf_op jit(solution)/shard_map/ppermute | solution.py:66
  194.4 73.1 %collective-permute-start.34 = (bf16[2304,512]{1,0:T(8,128)(2,1)}, bf16[2304,512]{1,0:T(8,128)(2,1)}, u32[]{:S(2)}, u32[]{:S(2)}) collective-permute-start(bf16[2304,512]{1,0:T(8,128)(2,1)} %bitcast.165), channel_id=1, source_target_pairs={{0,1},{1,0},{2,3},{3,2},{4,5},{5,4},{6,7},{7,6},{8,9},{9,8},{10,11... | collective-permute-start | bytes 7077896 | tf_op jit(solution)/shard_map/ppermute | solution.py:66
  255.5 159.8 %collective-permute-start.24 = (bf16[512,4608]{1,0:T(8,128)(2,1)}, bf16[512,4608]{1,0:T(8,128)(2,1)}, u32[]{:S(2)}, u32[]{:S(2)}) collective-permute-start(bf16[512,4608]{1,0:T(8,128)(2,1)} %bitcast.121), channel_id=1, source_target_pairs={{0,1},{1,0},{2,3},{3,2},{4,5},{5,4},{6,7},{7,6},{8,9},{9,8},{10,11... | collective-permute-start | bytes 14155784 | tf_op jit(solution)/shard_map/ppermute | solution.py:66
  262.1 176.1 %collective-permute-start.29 = (bf16[512,4608]{1,0:T(8,128)(2,1)}, bf16[512,4608]{1,0:T(8,128)(2,1)}, u32[]{:S(2)}, u32[]{:S(2)}) collective-permute-start(bf16[512,4608]{1,0:T(8,128)(2,1)} %bitcast.146), channel_id=1, source_target_pairs={{0,1},{1,0},{2,3},{3,2},{4,5},{5,4},{6,7},{7,6},{8,9},{9,8},{10,11... | collective-permute-start | bytes 14155784 | tf_op jit(solution)/shard_map/ppermute | solution.py:66
  835.1 37.4 %collective-permute-start.42 = (bf16[1024,512]{1,0:T(8,128)(2,1)}, bf16[1024,512]{1,0:T(8,128)(2,1)}, u32[]{:S(2)}, u32[]{:S(2)}) collective-permute-start(bf16[1024,512]{1,0:T(8,128)(2,1)} %bitcast.209), channel_id=1, source_target_pairs={{0,16},{8,24},{16,0},{24,8},{1,17},{9,25},{17,1},{25,9},{2,18},{10... | collective-permute-start | bytes 3145736 | tf_op jit(solution)/shard_map/ppermute | solution.py:66
  842.1 28.1 %collective-permute-start.40 = (bf16[1024,512]{1,0:T(8,128)(2,1)}, bf16[1024,512]{1,0:T(8,128)(2,1)}, u32[]{:S(2)}, u32[]{:S(2)}) collective-permute-start(bf16[1024,512]{1,0:T(8,128)(2,1)} %bitcast.201), channel_id=1, source_target_pairs={{0,8},{8,0},{16,24},{24,16},{1,9},{9,1},{17,25},{25,17},{2,10},{10... | collective-permute-start | bytes 3145736 | tf_op jit(solution)/shard_map/ppermute | solution.py:66
  845.8 29.8 %collective-permute-start.49 = (bf16[512,1024]{1,0:T(8,128)(2,1)}, bf16[512,1024]{1,0:T(8,128)(2,1)}, u32[]{:S(2)}, u32[]{:S(2)}) collective-permute-start(bf16[512,1024]{1,0:T(8,128)(2,1)} %bitcast.216), channel_id=1, source_target_pairs={{0,1},{1,0},{2,3},{3,2},{4,5},{5,4},{6,7},{7,6},{8,9},{9,8},{10,11... | collective-permute-start | bytes 3145736 | tf_op jit(solution)/shard_map/ppermute | solution.py:66
  849.3 91.2 %collective-permute-start.59 = (bf16[512,1024]{1,0:T(8,128)(2,1)}, bf16[512,1024]{1,0:T(8,128)(2,1)}, u32[]{:S(2)}, u32[]{:S(2)}) collective-permute-start(bf16[512,1024]{1,0:T(8,128)(2,1)} %bitcast.246), channel_id=1, source_target_pairs={{0,1},{1,0},{2,3},{3,2},{4,5},{5,4},{6,7},{7,6},{8,9},{9,8},{10,11... | collective-permute-start | bytes 3145736 | tf_op jit(solution)/shard_map/ppermute | solution.py:66
  868.0 69.3 %collective-permute-start.79 = (bf16[2304,512]{1,0:T(8,128)(2,1)}, bf16[2304,512]{1,0:T(8,128)(2,1)}, u32[]{:S(2)}, u32[]{:S(2)}) collective-permute-start(bf16[2304,512]{1,0:T(8,128)(2,1)} %bitcast.306), channel_id=1, source_target_pairs={{0,1},{1,0},{2,3},{3,2},{4,5},{5,4},{6,7},{7,6},{8,9},{9,8},{10,11... | collective-permute-start | bytes 7077896 | tf_op jit(solution)/shard_map/ppermute | solution.py:66
  870.1 75.0 %collective-permute-start.74 = (bf16[2304,512]{1,0:T(8,128)(2,1)}, bf16[2304,512]{1,0:T(8,128)(2,1)}, u32[]{:S(2)}, u32[]{:S(2)}) collective-permute-start(bf16[2304,512]{1,0:T(8,128)(2,1)} %bitcast.291), channel_id=1, source_target_pairs={{0,1},{1,0},{2,3},{3,2},{4,5},{5,4},{6,7},{7,6},{8,9},{9,8},{10,11... | collective-permute-start | bytes 7077896 | tf_op jit(solution)/shard_map/ppermute | solution.py:66
  875.5 15.9 %collective-permute-start.43 = (bf16[512,512]{1,0:T(8,128)(2,1)}, bf16[512,512]{1,0:T(8,128)(2,1)}, u32[]{:S(2)}, u32[]{:S(2)}) collective-permute-start(bf16[512,512]{1,0:T(8,128)(2,1)} %dynamic-slice_bitcast_fusion), channel_id=1, source_target_pairs={{0,8},{8,0},{16,24},{24,16},{1,9},{9,1},{17,25},{25,17},{2,10},{10... | collective-permute-start | bytes 1572872 | tf_op jit(solution)/shard_map/ppermute | solution.py:66
  905.0 19.4 %collective-permute-start.51 = (bf16[128,1024]{1,0:T(8,128)(2,1)S(1)}, bf16[128,1024]{1,0:T(8,128)(2,1)S(1)}, u32[]{:S(2)}, u32[]{:S(2)}) collective-permute-start(bf16[128,1024]{1,0:T(8,128)(2,1)S(1)} %bitcast.907), channel_id=1, source_target_pairs={{0,16},{8,24},{16,0},{24,8},{1,17},{9,25},{17,1},{25,9},{2,18},{10... | collective-permute-start | bytes 786440 | tf_op jit(solution)/shard_map/ppermute | solution.py:66
  924.4 16.8 %collective-permute-start.54 = (bf16[512,1024]{1,0:T(8,128)(2,1)S(1)}, bf16[512,1024]{1,0:T(8,128)(2,1)S(1)}, u32[]{:S(2)}, u32[]{:S(2)}) collective-permute-start(bf16[512,1024]{1,0:T(8,128)(2,1)S(1)} %bitcast.866), channel_id=1, source_target_pairs={{0,1},{1,0},{2,3},{3,2},{4,5},{5,4},{6,7},{7,6},{8,9},{9,8},{10,11... | collective-permute-start | bytes 3145736 | tf_op jit(solution)/shard_map/ppermute | solution.py:66
  936.7 108.8 %collective-permute-start.69 = (bf16[512,4608]{1,0:T(8,128)(2,1)S(1)}, bf16[512,4608]{1,0:T(8,128)(2,1)}, u32[]{:S(2)}, u32[]{:S(2)}) collective-permute-start(bf16[512,4608]{1,0:T(8,128)(2,1)S(1)} %bitcast.798), channel_id=1, source_target_pairs={{0,1},{1,0},{2,3},{3,2},{4,5},{5,4},{6,7},{7,6},{8,9},{9,8},{10,11... | collective-permute-start | bytes 14155784 | tf_op jit(solution)/shard_map/ppermute | solution.py:66
  937.4 108.1 %collective-permute-start.64 = (bf16[512,4608]{1,0:T(8,128)(2,1)}, bf16[512,4608]{1,0:T(8,128)(2,1)}, u32[]{:S(2)}, u32[]{:S(2)}) collective-permute-start(bf16[512,4608]{1,0:T(8,128)(2,1)} %bitcast.799), channel_id=1, source_target_pairs={{0,1},{1,0},{2,3},{3,2},{4,5},{5,4},{6,7},{7,6},{8,9},{9,8},{10,11... | collective-permute-start | bytes 14155784 | tf_op jit(solution)/shard_map/ppermute | solution.py:66
  940.5 90.0 %collective-permute-start.80 = (bf16[1152,512]{1,0:T(8,128)(2,1)S(1)}, bf16[1152,512]{1,0:T(8,128)(2,1)}, u32[]{:S(2)}, u32[]{:S(2)}) collective-permute-start(bf16[1152,512]{1,0:T(8,128)(2,1)S(1)} %bitcast.849), channel_id=1, source_target_pairs={{0,16},{8,24},{16,0},{24,8},{1,17},{9,25},{17,1},{25,9},{2,18},{10... | collective-permute-start | bytes 3538952 | tf_op jit(solution)/shard_map/ppermute | solution.py:66
  944.3 36.3 %collective-permute-start.55 = (bf16[256,1024]{1,0:T(8,128)(2,1)S(1)}, bf16[256,1024]{1,0:T(8,128)(2,1)S(1)}, u32[]{:S(2)}, u32[]{:S(2)}) collective-permute-start(bf16[256,1024]{1,0:T(8,128)(2,1)S(1)} %bitcast.898), channel_id=1, source_target_pairs={{0,16},{8,24},{16,0},{24,8},{1,17},{9,25},{17,1},{25,9},{2,18},{10... | collective-permute-start | bytes 1572872 | tf_op jit(solution)/shard_map/ppermute | solution.py:66
  945.1 45.8 %collective-permute-start.60 = (bf16[256,1024]{1,0:T(8,128)(2,1)S(1)}, bf16[256,1024]{1,0:T(8,128)(2,1)S(1)}, u32[]{:S(2)}, u32[]{:S(2)}) collective-permute-start(bf16[256,1024]{1,0:T(8,128)(2,1)S(1)} %bitcast.897), channel_id=1, source_target_pairs={{0,16},{8,24},{16,0},{24,8},{1,17},{9,25},{17,1},{25,9},{2,18},{10... | collective-permute-start | bytes 1572872 | tf_op jit(solution)/shard_map/ppermute | solution.py:66
  980.6 54.7 %collective-permute-start.75 = (bf16[1152,512]{1,0:T(8,128)(2,1)S(1)}, bf16[1152,512]{1,0:T(8,128)(2,1)S(1)}, u32[]{:S(2)}, u32[]{:S(2)}) collective-permute-start(bf16[1152,512]{1,0:T(8,128)(2,1)S(1)} %bitcast.846), channel_id=1, source_target_pairs={{0,8},{8,0},{16,24},{24,16},{1,9},{9,1},{17,25},{25,17},{2,10},{10... | collective-permute-start | bytes 3538952 | tf_op jit(solution)/shard_map/ppermute | solution.py:66
  990.9 21.5 %collective-permute-start.56 = (bf16[128,1024]{1,0:T(8,128)(2,1)S(1)}, bf16[128,1024]{1,0:T(8,128)(2,1)S(1)}, u32[]{:S(2)}, u32[]{:S(2)}) collective-permute-start(bf16[128,1024]{1,0:T(8,128)(2,1)S(1)} %bitcast.908), channel_id=1, source_target_pairs={{0,8},{8,0},{16,24},{24,16},{1,9},{9,1},{17,25},{25,17},{2,10},{10... | collective-permute-start | bytes 786440 | tf_op jit(solution)/shard_map/ppermute | solution.py:66
  1037.3 15.7 %collective-permute-start.76 = (bf16[576,512]{1,0:T(8,128)(2,1)}, bf16[576,512]{1,0:T(8,128)(2,1)}, u32[]{:S(2)}, u32[]{:S(2)}) collective-permute-start(bf16[576,512]{1,0:T(8,128)(2,1)} %bitcast.297), channel_id=1, source_target_pairs={{0,16},{8,24},{16,0},{24,8},{1,17},{9,25},{17,1},{25,9},{2,18},{10... | collective-permute-start | bytes 1769480 | tf_op jit(solution)/shard_map/ppermute | solution.py:66
  1052.1 44.6 %collective-permute-start.65 = (bf16[256,4608]{1,0:T(8,128)(2,1)S(1)}, bf16[256,4608]{1,0:T(8,128)(2,1)S(1)}, u32[]{:S(2)}, u32[]{:S(2)}) collective-permute-start(bf16[256,4608]{1,0:T(8,128)(2,1)S(1)} %bitcast.822), channel_id=1, source_target_pairs={{0,8},{8,0},{16,24},{24,16},{1,9},{9,1},{17,25},{25,17},{2,10},{10... | collective-permute-start | bytes 7077896 | tf_op jit(solution)/shard_map/ppermute | solution.py:66
  1064.8 54.2 %collective-permute-start.70 = (bf16[256,4608]{1,0:T(8,128)(2,1)S(1)}, bf16[256,4608]{1,0:T(8,128)(2,1)S(1)}, u32[]{:S(2)}, u32[]{:S(2)}) collective-permute-start(bf16[256,4608]{1,0:T(8,128)(2,1)S(1)} %bitcast.826), channel_id=1, source_target_pairs={{0,16},{8,24},{16,0},{24,8},{1,17},{9,25},{17,1},{25,9},{2,18},{10... | collective-permute-start | bytes 7077896 | tf_op jit(solution)/shard_map/ppermute | solution.py:66
  1097.5 34.2 %collective-permute-start.66 = (bf16[128,4608]{1,0:T(8,128)(2,1)S(1)}, bf16[128,4608]{1,0:T(8,128)(2,1)S(1)}, u32[]{:S(2)}, u32[]{:S(2)}) collective-permute-start(bf16[128,4608]{1,0:T(8,128)(2,1)S(1)} %bitcast.847), channel_id=1, source_target_pairs={{0,16},{8,24},{16,0},{24,8},{1,17},{9,25},{17,1},{25,9},{2,18},{10... | collective-permute-start | bytes 3538952 | tf_op jit(solution)/shard_map/ppermute | solution.py:66
  1119.8 16.3 %collective-permute-start.71 = (bf16[128,4608]{1,0:T(8,128)(2,1)S(1)}, bf16[128,4608]{1,0:T(8,128)(2,1)S(1)}, u32[]{:S(2)}, u32[]{:S(2)}) collective-permute-start(bf16[128,4608]{1,0:T(8,128)(2,1)S(1)} %bitcast.848), channel_id=1, source_target_pairs={{0,8},{8,0},{16,24},{24,16},{1,9},{9,1},{17,25},{25,17},{2,10},{10... | collective-permute-start | bytes 3538952 | tf_op jit(solution)/shard_map/ppermute | solution.py:66
  1136.4 20.6 %collective-permute-start.72 = (bf16[64,4608]{1,0:T(8,128)(2,1)S(1)}, bf16[64,4608]{1,0:T(8,128)(2,1)S(1)}, u32[]{:S(2)}, u32[]{:S(2)}) collective-permute-start(bf16[64,4608]{1,0:T(8,128)(2,1)S(1)} %bitcast.879), channel_id=1, source_target_pairs={{0,2},{1,3},{2,0},{3,1},{4,6},{5,7},{6,4},{7,5},{8,10},{9,11},{10,... | collective-permute-start | bytes 1769480 | tf_op jit(solution)/shard_map/ppermute | solution.py:66
  (227 other events, 1682.7 us)
Sparse Core Ops, SparseCore 0:
  123.9 89.5 all-gather.1
